TPU v7x, 256 devices: a whole 4x4x8 slice. The times are simulated.
256 devices in a mesh: row: 8 (over z_hi, x), col: 32 (over y, z_lo, core).
Axes of the slice: x: 4, y: 4, z: 8 (z_hi: 2, z_lo: 4; z = z_hi * 4 + z_lo), core: 2. Of those that a mesh axis runs over, the one named last changes fastest.
Arguments:
- projector: float32 [18432, 18432], P('row', 'col'), may hold values from -9 to 490, as said below
- saved: float32 [18432, 512], P('col', 'row'), may hold values from -0.0048828125 to 0.0048828125
- grad_slab: float32 [512, 18432], P('col', 'row'), may hold values from -0.03125 to 0.03125
Outputs:
- updated: float32 [18432, 18432], P('row', 'col')
- projected: float32 [512, 18432], P('row', 'col')
Inputs may be any that keep to these rules, and one draw needn't show every extreme that they name: projector is symmetric and positive definite, every eigenvalue above 100; its diagonal entries lie between 390 and 490.
All inputs are finite; a program needn't handle non-finite values.
Results may differ from a plain program's by a relative error of at most 0.000071.
Values sent between devices are 32-bit elements; how exact they have to be, the bound alone decides.
A program may use at most 128 MiB of HBM per device.

v0:
```python
import jax
import jax.numpy as jnp
from jax import lax
from jax.sharding import PartitionSpec as P


def broadcast(block, axis, source):
    block = jnp.where(lax.axis_index(axis) == source, block, jnp.zeros_like(block))
    return lax.psum(block, axis)


def local(projector, saved, grad_slab):
    highest = lax.Precision.HIGHEST
    cols_block = projector.shape[1]
    per_row = lax.axis_size("col") // lax.axis_size("row")
    col_index = lax.axis_index("col")
    owner_row = col_index // per_row
    offset = col_index % per_row * cols_block
    saved_cols = lax.all_gather(saved, "row", axis=1, tiled=True)
    partial_value = jnp.dot(
        projector, saved_cols, precision=highest, preferred_element_type=jnp.float32
    )
    y_rows = lax.psum(partial_value, "col")
    own_slice = lax.dynamic_slice_in_dim(y_rows, offset, cols_block, 0)
    y_cols = broadcast(own_slice, "row", owner_row)
    gram_term = jnp.dot(saved_cols.T, y_cols, precision=highest, preferred_element_type=jnp.float32)
    gram_total = lax.psum(gram_term, "col")
    system = jnp.eye(saved_cols.shape[1], dtype=jnp.float32) + gram_total
    factor = jnp.linalg.cholesky(system)
    solved = jax.scipy.linalg.cho_solve((factor, True), y_cols.T)
    updated = projector - jnp.dot(
        y_rows, solved, precision=highest, preferred_element_type=jnp.float32
    )
    row_terms = jnp.dot(
        lax.all_gather(grad_slab, "col", axis=0, tiled=True),
        updated,
        precision=highest,
        preferred_element_type=jnp.float32,
    )
    projected = lax.psum_scatter(row_terms, "row", scatter_dimension=0, tiled=True)
    return (updated, projected)


def solution(mesh):
    return jax.shard_map(
        local,
        mesh=mesh,
        in_specs=(P("row", "col"), P("col", "row"), P("col", "row")),
        out_specs=(P("row", "col"), P("row", "col")),
        check_vma=False,
    )
```

profile of v0, /device:TPU:1, one launch (start us, length us, event | category | flops | bytes accessed | tf_op | source)
XLA Modules:
  0.0 1070.7 jit_solution(394723281427311639)
XLA Ops:
  7.2 0.7 all-gather.3.cloned.1.call-update
  7.9 70.6 %all-gather.3.cloned.1.call-done = f32[576,512]{0,1:T(8,128)} async-done(((f32[576,64]{0,1:T(8,128)}), f32[576,512]{0,1:T(8,128)}) %all-gather.3.cloned.1.call-update) | async-done | bytes 1179664 | tf_op jit(solution)/shard_map/all_gather | solution.py:19
  78.6 22.2 %fusion.56 = f32[2304,512]{1,0:T(8,128)} fusion(f32[2304,576]{0,1:T(8,128)} %param.3, f32[576,512]{0,1:T(8,128)} %all-gather.3.cloned.1.call-done), kind=kOutput, calls=%fused_computation.100 | convolution fusion | flops 8153726976 | bytes 11206656 | tf_op jit(solution)/shard_map/dot_general | solution.py:20
  100.9 291.8 %all-reduce.5.cloned.1.call-done = f32[2304,512]{1,0:T(8,128)} async-done(((f32[2304,512]{1,0:T(8,128)}), f32[2304,512]{1,0:T(8,128)}) %all-reduce.5.cloned.1.call-update) | async-done | bytes 4718608 | tf_op jit(solution)/shard_map/psum | solution.py:23
  392.7 2.4 dynamic-slice_select_fusion
  395.5 109.9 %all-reduce.7.cloned.1.call-done = f32[576,512]{1,0:T(8,128)} async-done(((f32[576,512]{1,0:T(8,128)}), f32[576,512]{1,0:T(8,128)}) %all-reduce.7.cloned.1.call-update) | async-done | bytes 1179664 | tf_op jit(solution)/shard_map/psum | solution.py:9
  505.4 6.6 convolution_bitcast_fusion.1
  512.0 0.5 all-gather.5.cloned.1.call-update
  512.6 279.1 %all-reduce.9.cloned.1.call-done = f32[512,512]{0,1:T(8,128)} async-done(((f32[512,512]{0,1:T(8,128)}), f32[512,512]{0,1:T(8,128)}) %all-reduce.9.cloned.1.call-update) | async-done | bytes 1048592 | tf_op jit(solution)/shard_map/psum | solution.py:27
  791.8 1.3 convert_add_fusion
  793.4 0.9 copy-done.3
  794.6 11.7 %cholesky.104 = f32[128,128]{1,0:T(8,128)S(1)} custom-call(f32[128,128]{1,0:T(8,128)S(1)} %cholesky.266), custom_call_target="Cholesky" | custom-call | tf_op jit(solution)/shard_map/jit(cholesky)/cholesky | solution.py:29
  806.5 9.8 custom-call.34
  816.9 11.7 %cholesky.217 = f32[128,128]{1,0:T(8,128)S(1)} custom-call(f32[128,128]{1,0:T(8,128)S(1)} %cholesky.270), custom_call_target="Cholesky" | custom-call | tf_op jit(solution)/shard_map/jit(cholesky)/cholesky | solution.py:29
  828.7 18.5 %custom-call.35 = f32[1,128,128]{1,2,0:T(8,128)S(1)} custom-call(f32[1,128,128]{2,1,0:T(8,128)S(1)} %get-tuple-element.30), custom_call_target="InvertDiagBlocksLowerTriangular" | custom-call | tf_op jit(solution)/shard_map/jit(cholesky)/cholesky | solution.py:29
  847.9 11.7 %cholesky.238 = f32[128,128]{1,0:T(8,128)S(1)} custom-call(f32[128,128]{1,0:T(8,128)S(1)} %cholesky.275), custom_call_target="Cholesky" | custom-call | tf_op jit(solution)/shard_map/jit(cholesky)/cholesky | solution.py:29
  859.6 9.8 custom-call.36
  869.7 1.3 convolution_subtract_fusion.9
  871.0 11.7 %cholesky.255 = f32[128,128]{1,0:T(8,128)S(1)} custom-call(f32[128,128]{1,0:T(8,128)S(1)} %convolution_subtract_fusion.9), custom_call_target="Cholesky" | custom-call | tf_op jit(solution)/shard_map/jit(cholesky)/cholesky | solution.py:29
  882.7 0.7 compare_reduce_fusion.2
  884.6 0.6 compare_reduce_fusion.1
  886.0 0.8 compare_reduce_fusion
  887.4 1.1 select_select_fusion
  888.5 13.6 %while.1 = (s32[]{:T(128)}, f32[512,512]{1,0:T(8,128)}, s32[4,2]{0,1:T(2,128)S(1)}, f32[4,128,128]{2,1,0:T(8,128)}, s32[]{:T(128)}) while((s32[]{:T(128)}, f32[512,512]{1,0:T(8,128)}, s32[4,2]{0,1:T(2,128)S(1)}, f32[4,128,128]{2,1,0:T(8,128)}, s32[]{:T(128)}) %tuple.33), condition=%wide.while_cond, body=%wide.while_body.sunk | while | flops 2 | bytes 132705 | solution.py:30
  888.6 0.5 fusion.75
  889.1 2.8 bitcast_dynamic-update-slice_fusion.2
  892.0 0.5 fusion.75
  892.5 2.8 bitcast_dynamic-update-slice_fusion.2
  895.4 0.5 fusion.75
  896.0 2.8 bitcast_dynamic-update-slice_fusion.2
  898.8 0.5 fusion.75
  899.4 2.8 bitcast_dynamic-update-slice_fusion.2
  902.1 40.8 %custom-call.37 = f32[4,128,128]{1,2,0:T(8,128)} custom-call(f32[4,128,128]{2,1,0:T(8,128)} %get-tuple-element.9), custom_call_target="InvertDiagBlocksLowerTriangular" | custom-call | tf_op jit(solution)/shard_map/jit(_cho_solve)/triangular_solve | solution.py:30
  943.0 1.3 fusion.24
  944.3 1.2 convolution_subtract_fusion.4
  945.9 0.6 convolution_subtract_fusion.3
  947.0 0.9 convolution_subtract_fusion.6
  948.0 0.5 fusion.49
  948.5 0.7 fusion.48
  949.6 0.4 fusion.46
  950.0 0.6 convolution_subtract_fusion.1
  950.6 0.4 fusion.44
  951.0 0.9 convolution_subtract_fusion.5
  951.9 0.4 fusion.43
  952.4 12.3 %convolution_subtract_fusion = f32[2304,576]{0,1:T(8,128)} fusion(f32[2304,576]{0,1:T(8,128)S(1)} %bitcast.71, f32[2304,512]{1,0:T(8,128)} %all-reduce.5.cloned.1.call-done, f32[128,576]{0,1:T(8,128)S(1)} %fusion.48, f32[128,576]{0,1:T(8,128)S(1)} %fusion.46, f32[128,576]{0,1:T(8,128)S(1)} %fusion.44, f32[128,576]{0,1:T(8,128)S(1)} %fusion.43), kind=kOutput, calls=%fused_computation.2 | convolution fusion | flops 8155938816 | bytes 16515072 | tf_op jit(solution)/shard_map/dot_general | solution.py:31
  964.7 10.9 %convolution_bitcast_fusion = f32[512,576]{0,1:T(8,128)S(1)} fusion(f32[2304,576]{0,1:T(8,128)} %convolution_subtract_fusion, f32[512,2304]{1,0:T(8,128)} %all-gather.5.cloned.1.call-done), kind=kOutput, calls=%fused_computation.3 | convolution fusion | flops 8153726976 | bytes 11206656 | tf_op jit(solution)/shard_map/dot_general | solution.py:34
  975.6 1.5 copy.9
  977.1 86.3 %reduce-scatter.4.cloned.1.call-done = f32[64,576]{1,0:T(8,128)} async-done(((f32[512,576]{1,0:T(8,128)}), f32[64,576]{1,0:T(8,128)}) %reduce-scatter.4.cloned.1.call-update) | async-done | bytes 147472
  (52 shorter events, 4.4 us)
Async XLA Ops:
  7.2 71.4 %all-gather.3.cloned.1.call-start = ((), (), s32[]{:S(2)}) async-start(), calls=%async_computation.1 | async-start | bytes 1474560 | tf_op jit(solution)/shard_map/all_gather | solution.py:19
  7.9 384.8 %all-reduce.5.cloned.1.call-start = ((), (), s32[]{:S(2)}) async-start(), calls=%async_computation.2 | async-start | bytes 9437184 | tf_op jit(solution)/shard_map/psum | solution.py:23
  100.8 404.6 %all-reduce.7.cloned.1.call-start = ((), (), s32[]{:S(2)}) async-start(), calls=%async_computation.3 | async-start | bytes 2359296 | tf_op jit(solution)/shard_map/psum | solution.py:9
  100.9 404.5 %copy-start = (f32[576,512]{0,1:T(8,128)S(1)}, f32[576,512]{0,1:T(8,128)}, u32[]{:S(2)}) copy-start(f32[576,512]{0,1:T(8,128)} %all-gather.3.cloned.1.call-done) | copy-start | bytes 3538948
  395.2 396.6 %all-reduce.9.cloned.1.call-start = ((), (), s32[]{:S(2)}) async-start(), calls=%async_computation.4 | async-start | bytes 2097152 | tf_op jit(solution)/shard_map/psum | solution.py:27
  512.0 452.7 %all-gather.5.cloned.1.call-start = ((), (), s32[]{:S(2)}) async-start(), calls=%async_computation.5 | async-start | bytes 4866048 | tf_op jit(solution)/shard_map/all_gather | solution.py:35
  512.6 550.8 %reduce-scatter.4.cloned.1.call-start = ((), (), s32[]{:S(2)}) async-start(), calls=%async_computation.6 | async-start | bytes 1474560
  793.1 1.2 copy-start.3
  794.5 52.9 %copy-start.4 = (f32[512,512]{1,0:T(8,128)}, f32[512,512]{1,0:T(8,128)S(1)}, u32[]{:S(2)}) copy-start(f32[512,512]{1,0:T(8,128)S(1)} %fusion.7) | copy-start | bytes 3145732
  869.7 73.3 %copy-start.1 = (f32[576,512]{1,0:T(8,128)S(1)}, f32[576,512]{1,0:T(8,128)}, u32[]{:S(2)}) copy-start(f32[576,512]{1,0:T(8,128)} %all-reduce.7.cloned.1.call-done) | copy-start | bytes 3538948
  887.4 65.0 %slice-start = ((s8[5308416]{0:T(1024)(128)(4,1)}), s8[1114112]{0:T(1024)(128)(4,1)S(1)}, s32[]{:S(2)}) async-start(s8[5308416]{0:T(1024)(128)(4,1)} %bitcast.70), calls=%async_computation.7 | async-start | bytes 2228224
  902.1 43.8 %copy-start.2 = (f32[512,512]{1,0:T(8,128)S(1)}, f32[512,512]{1,0:T(8,128)}, u32[]{:S(2)}) copy-start(f32[512,512]{1,0:T(8,128)} %get-tuple-element.98) | copy-start | bytes 3145732
  943.0 2.6 copy-start.5
  947.0 5.4 slice-start.1
Sparse Core Ops, SparseCore 0:
  10.6 67.9 all-gather.2
  100.9 291.7 all-reduce.4
  396.0 109.3 all-reduce.6
  512.1 279.6 all-reduce.8
  793.6 63.9 all-gather.4
  977.2 86.1 reduce-scatter.3
where the time goes:
time: 1080 us; the launch traced here: 1070 us
  waiting for transfers between devices  839 us (78%)
  other arithmetic  133 us (12%)
  matrix products  64.1 us (6%)
  between operations  17.5 us (2%)
  local copies, waits for them, and re-layouts  16.5 us (2%)
    psum x1, waiting for transfers between devices, local(): y_rows = lax.psum(partial_value, 'col')  292 us
    psum x1, waiting for transfers between devices, local(): gram_total = lax.psum(gram_term, 'col')  279 us
    psum x1, waiting for transfers between devices, broadcast(): return lax.psum(block, axis)  110 us
    unnamed x7, waiting for transfers between devices  87.6 us
    another operation x14, other arithmetic, local(): factor = jnp.linalg.cholesky(system)  87.2 us
    all_gather x1, waiting for transfers between devices, local(): saved_cols = lax.all_gather(saved, 'row', axis=1, tiled=True)  70.6 us
    another operation x3, other arithmetic, local(): solved = jax.scipy.linalg.cho_solve((factor, True), y_cols.T)  41.9 us
    dot_general x1, matrix products, local(): jnp.dot(projector, saved_cols, precision=highest, preferred_element_type=...  22.2 us
  transfers between devices with their start and end apart: 6, of which 5 were waited for; matrix products, arithmetic and copies ran while one was open for 16% of the time, Pallas kernels for 0%

commit v1 on v0

v1 whole, which is shorter than its diff:
```python
import functools

import jax
import jax.numpy as jnp
from jax import lax
from jax.experimental import pallas as pl
from jax.experimental.pallas import tpu as pltpu
from jax.sharding import PartitionSpec as P

MESH = pl.DeviceIdType.MESH
F32 = jnp.float32
BF16 = jnp.bfloat16
NN = (((1,), (0,)), ((), ()))
NT = (((1,), (1,)), ((), ()))
TN = (((0,), (0,)), ((), ()))


def split(x):
    hi = x.astype(BF16)
    return hi, (x - hi.astype(F32)).astype(BF16)


def dot3(a_hi, a_lo, b_hi, b_lo, dims=NN):
    dot = functools.partial(lax.dot_general, dimension_numbers=dims, preferred_element_type=F32)
    return dot(a_hi, b_hi) + (dot(a_hi, b_lo) + dot(a_lo, b_hi))


def dot_full(a, b, dims=NN):
    return lax.dot_general(a, b, dims, precision=lax.Precision.HIGHEST, preferred_element_type=F32)


class Place:
    def __init__(self):
        self.row = lax.axis_index("row")
        self.col = lax.axis_index("col")
        self.zh = self.row // 4
        self.x = self.row % 4
        self.y = self.col // 8
        self.zl = (self.col // 2) % 4
        self.k = self.col % 2

    def at(self, zh=None, x=None, y=None, zl=None, k=None):
        zh = self.zh if zh is None else zh
        x = self.x if x is None else x
        y = self.y if y is None else y
        zl = self.zl if zl is None else zl
        k = self.k if k is None else k
        return (zh * 4 + x, y * 8 + zl * 2 + k)

    def sib(self):
        return self.at(k=1 - self.k)

    def anti(self):
        return self.at(zh=1 - self.zh)

    def xd(self, d):
        return self.at(x=(self.x + d) % 4)

    def yd(self, d):
        return self.at(y=(self.y + d) % 4)

    def zd(self, d):
        return self.at(zl=(self.zl + d) % 4)

    def strip(self, q):
        return (self.col // 4, 8 * (self.col % 4) + q)

    def strip_source(self, r):
        return (r, 4 * self.row + self.col // 8)

    def is_me(self, dev):
        return jnp.logical_and(dev[0] == self.row, dev[1] == self.col)


class Links:
    def __init__(self, me, send, recv):
        self.me, self.send, self.recv, self.used = me, send, recv, 0
        self.sent = []

    def slot(self, n=1):
        self.used += n
        assert self.used <= NSEM, self.used
        return self.used - n

    def push(self, src, dst, dev):
        i = self.slot()
        copy = pltpu.make_async_remote_copy(
            src_ref=src, dst_ref=dst, send_sem=self.send.at[i], recv_sem=self.recv.at[i],
            device_id=dev, device_id_type=MESH)
        copy.start()
        self.sent.append(copy)
        return copy

    def finish(self):
        for copy in self.sent:
            copy.wait_send()


NSEM = 160


class PlaneGather:
    def __init__(self, links, buf):
        self.links, self.buf, self.me = links, buf, links.me

    def start(self):
        me, buf = self.me, self.buf
        mine = buf.at[me.y, me.zl, me.k]
        self.z = [self.links.push(mine, mine, me.zd(d)) for d in (1, 2, 3)]

    def pair(self, y):
        part = self.buf.at[y, :, self.me.k]
        self.pairs.append(self.links.push(part, part, self.me.sib()))

    def step1(self):
        me, buf = self.me, self.buf
        self.pairs = []
        for copy in self.z:
            copy.wait_recv()
        mine = buf.at[me.y, :, me.k]
        self.up = self.links.push(mine, mine, me.yd(1))
        self.down = self.links.push(mine, mine, me.yd(3))
        self.pair(me.y)

    def step2(self):
        me, buf = self.me, self.buf
        below, above = (me.y + 3) % 4, (me.y + 1) % 4
        self.up.wait_recv()
        half = buf.at[below, pl.ds(0, 2), me.k]
        self.up2 = self.links.push(half, half, me.yd(1))
        self.down.wait_recv()
        half = buf.at[above, pl.ds(2, 2), me.k]
        self.down2 = self.links.push(half, half, me.yd(3))
        self.pair(below)
        self.pair(above)

    def step3(self):
        self.up2.wait_recv()
        self.down2.wait_recv()
        self.pair((self.me.y + 2) % 4)

    def finish(self):
        for copy in self.pairs:
            copy.wait_recv()


class RowGather:
    def __init__(self, links, buf):
        self.links, self.buf, self.me = links, buf, links.me

    def start(self):
        me = self.me
        mine = self.buf.at[me.row]
        self.far = self.links.push(mine, mine, me.anti())
        self.near = [self.links.push(mine, mine, me.xd(d)) for d in (1, 2, 3)]

    def step(self):
        me = self.me
        self.far.wait_recv()
        other = self.buf.at[(me.row + 4) % 8]
        self.near2 = [self.links.push(other, other, me.xd(d)) for d in (1, 2, 3)]

    def finish(self):
        for copy in self.near + self.near2:
            copy.wait_recv()


def barrier(me):
    sem = pltpu.get_barrier_semaphore()
    devs = [me.sib(), me.anti()]
    devs += [f(d) for f in (me.xd, me.yd, me.zd) for d in (1, 2, 3)]
    for dev in devs:
        pl.semaphore_signal(sem, inc=1, device_id=dev, device_id_type=MESH)
    for dev in [me.strip_source(r) for r in range(8)] + [me.strip(me.row)]:

        @pl.when(jnp.logical_not(me.is_me(dev)))
        def _():
            pl.semaphore_signal(sem, inc=1, device_id=dev, device_id_type=MESH)

    count = jnp.int32(len(devs))
    for dev in [me.strip(q) for q in range(8)] + [me.strip_source(me.col % 8)]:
        count += jnp.where(me.is_me(dev), 0, 1)
    pl.semaphore_wait(sem, count)


class LooseCopy:
    def __init__(self, links, src, dst, dev, send, recv):
        me = links.me
        self.remote = pltpu.make_async_remote_copy(
            src_ref=src, dst_ref=dst, send_sem=links.send.at[send], recv_sem=links.recv.at[recv],
            device_id=dev, device_id_type=MESH)
        self.here = me.is_me(dev)
        self.local = pltpu.make_async_copy(src, dst, links.recv.at[recv])
        pl.when(jnp.logical_not(self.here))(lambda: self.remote.start())
        pl.when(self.here)(lambda: self.local.start())
        links.sent.append(self)

    def wait_send(self):
        pl.when(jnp.logical_not(self.here))(lambda: self.remote.wait_send())


def invert(a):
    n = a.shape[0]
    ri = lax.broadcasted_iota(jnp.int32, (n, n), 0)
    ci = lax.broadcasted_iota(jnp.int32, (n, n), 1)
    for k in range(n):
        row = a[k:k + 1, :]
        col = a[:, k:k + 1]
        p = 1.0 / a[k:k + 1, k:k + 1]
        rp = row * p
        b = jnp.where(ci == k, -(col * p), a - col * rp)
        a = jnp.where(ri == k, jnp.where(ci[0:1] == k, p, rp), b)
    return a


def mega(p_hbm, xp_ref, g_ref, yr_hbm, wt_ref, proj_ref,
         pst, p_hi, p_lo, xbuf, xs, xc_hi, xc_lo, gbuf, part, d2d, csum, r1, r2, rz, ybuf, ycb, x72,
         gram, gram_in, ga, gy_in, gb, gx_in, gc, gz_in, gout, amat, gpp, gpx, gps, gpa, gp64,
         gyp, gyd, gya, gyy, gyb, gyz, gyo, send, recv, lsem):
    me = Place()
    row, col, zh, x, y, zl, k = me.row, me.col, me.zh, me.x, me.y, me.zl, me.k
    links = Links(me, send, recv)
    pcopy = pltpu.make_async_copy(p_hbm, pst, lsem.at[0])
    pcopy.start()
    xbuf[row] = xp_ref[...]
    gbuf[y, zl, k] = g_ref[...]
    barrier(me)
    xg = RowGather(links, xbuf)
    xg.start()
    base_s, base_r = links.slot(8), links.slot(8)
    for q in range(8):
        LooseCopy(links, xp_ref.at[pl.ds(72 * (q % 4), 72)], xs.at[row], me.strip(q), base_s + q, base_r + row)
    gg = PlaneGather(links, gbuf)
    gg.start()
    pcopy.wait()

    @pl.loop(0, 36)
    def _(i):
        rows = pl.ds(pl.multiple_of(i * 64, 64), 64)
        p_hi[rows], p_lo[rows] = split(pst[rows])

    xg.step()
    gg.step1()
    lane = lax.broadcasted_iota(jnp.int32, (288, 128), 1)
    xg.finish()
    for m in range(4):
        b0, b1 = xbuf[2 * m], xbuf[2 * m + 1]
        cols = pl.ds(128 * m, 128)
        xc_hi[0:288, cols], xc_lo[0:288, cols] = split(jnp.where(lane < 64, b0, pltpu.roll(b1, 64, 1)))
        xc_hi[288:576, cols], xc_lo[288:576, cols] = split(jnp.where(lane < 64, pltpu.roll(b0, 64, 1), b1))

    def multiply(ay):
        @pl.loop(0, 4)
        def _(z):
            rows = pl.ds(pl.multiple_of(ay * 576 + z * 144, 144), 144)
            part[ay, z] = dot3(p_hi[rows], p_lo[rows], xc_hi[...], xc_lo[...]).reshape(2, 72, 512)
        return links.push(part.at[ay, :, 1 - k], d2d.at[ay], me.sib())

    def add_pair(ay, copy):
        copy.wait_recv()

        @pl.loop(0, 4)
        def _(z):
            csum[ay, z] = part[ay, z, k] + d2d[ay, z]

    y1, y2, y3 = (y + 1) % 4, (y + 2) % 4, (y + 3) % 4
    c2 = multiply(y2)
    c1 = multiply(y1)
    add_pair(y2, c2)
    up = links.push(csum.at[y2, pl.ds(0, 2)], r1.at[0], me.yd(1))
    down = links.push(csum.at[y2, pl.ds(2, 2)], r1.at[1], me.yd(3))
    c3 = multiply(y3)
    add_pair(y1, c1)
    c0 = multiply(y)
    add_pair(y3, c3)
    up.wait_recv()
    for z in range(2):
        csum[y1, z] += r1[0, z]
    up2 = links.push(csum.at[y1], r2.at[0], me.yd(1))
    down.wait_recv()
    for z in range(2):
        csum[y3, z + 2] += r1[1, z]
    down2 = links.push(csum.at[y3], r2.at[1], me.yd(3))
    add_pair(y, c0)

    for r in range(8):
        links_recv = pltpu.make_async_copy(xs.at[r], xs.at[r], recv.at[base_r + r])
        links_recv.wait()
    lane72 = lax.broadcasted_iota(jnp.int32, (72, 128), 1)
    flip = (col % 8) >= 4
    for m in range(4):
        b0, b1 = xs[2 * m], xs[2 * m + 1]
        first = jnp.where(lane72 < 64, b0, pltpu.roll(b1, 64, 1))
        second = jnp.where(lane72 < 64, pltpu.roll(b0, 64, 1), b1)
        x72[:, 128 * m:128 * m + 128] = jnp.where(flip, second, first)

    gg.step2()
    up2.wait_recv()
    down2.wait_recv()

    @pl.loop(0, 4)
    def _(z):
        csum[y, z] = csum[y, z] + (r2[0, z] + r2[1, z])

    zc = []
    for d in (1, 2, 3):
        zc.append(links.push(csum.at[y, (zl + d) % 4], rz.at[d - 1], me.zd(d)))
    gg.step3()
    for copy in zc:
        copy.wait_recv()
    y72 = csum[y, zl] + rz[0] + (rz[1] + rz[2])
    ybuf[y, zl, k] = y72
    yg = PlaneGather(links, ybuf)
    yg.start()
    yc = LooseCopy(links, ybuf.at[y, zl, k], ycb.at[col % 8], me.strip_source(col % 8), links.slot(), links.slot())

    yv = ybuf[y, zl, k]
    for i, (top, left) in enumerate(((0, 0), (128, 0), (128, 256), (0, 128))):
        g = dot_full(x72[:, 128 * i:128 * i + 128], yv[:, :128 * i + 128], TN)
        gram[top // 128, :, :, :, left:left + 128 * i + 128] = g.reshape(4, 4, 8, 128 * i + 128)
    copy = links.push(gram.at[1 - k], gram_in, me.sib())
    copy.wait_recv()
    for i in range(4):
        ga[i] = gram[k, i] + gram_in[i]
    cs = [links.push(ga.at[(y + d) % 4], gy_in.at[d - 1], me.yd(d)) for d in (1, 2, 3)]
    for copy in cs:
        copy.wait_recv()
    gb[...] = ga[y] + gy_in[0] + (gy_in[1] + gy_in[2])
    cs = [links.push(gb.at[(x + d) % 4], gx_in.at[d - 1], me.xd(d)) for d in (1, 2, 3)]
    for copy in cs:
        copy.wait_recv()
    gc[0] = gb[x] + gx_in[0] + (gx_in[1] + gx_in[2])
    cs = [links.push(gc.at[0], gz_in.at[d - 1], me.zd(d)) for d in (1, 2, 3)]
    for copy in cs:
        copy.wait_recv()
    gc[1] = gc[0] + gz_in[0] + (gz_in[1] + gz_in[2])
    copy = links.push(gc.at[1], gz_in.at[3], me.anti())
    copy.wait_recv()
    gout[k, y, x] = gc[1] + gz_in[3]
    cs = [links.push(gout.at[k, y, x], gout.at[k, y, x], me.xd(d)) for d in (1, 2, 3)]
    for copy in cs:
        copy.wait_recv()
    cs = [links.push(gout.at[k, y], gout.at[k, y], me.yd(d)) for d in (1, 2, 3)]
    for copy in cs:
        copy.wait_recv()
    copy = links.push(gout.at[k], gout.at[k], me.sib())
    yg.step1()
    yc.remote.wait_recv()
    ycg = RowGather(links, ycb)
    ycg.start()
    copy.wait_recv()

    ri = lax.broadcasted_iota(jnp.int32, (128, 128), 0)
    ci = lax.broadcasted_iota(jnp.int32, (128, 128), 1)
    for i, (top, left) in enumerate(((0, 0), (1, 0), (1, 256), (0, 128))):
        for j in range(i + 1):
            b = gout[top, :, :, :, left + 128 * j:left + 128 * j + 128].reshape(128, 128)
            if i == j:
                amat[128 * i:128 * i + 128, 128 * i:128 * i + 128] = b + jnp.where(ri == ci, 1.0, 0.0)
            else:
                amat[128 * i:128 * i + 128, 128 * j:128 * j + 128] = b
                amat[128 * j:128 * j + 128, 128 * i:128 * i + 128] = b.T

    def eliminate(j):
        at = pl.ds(pl.multiple_of(j * 128, 128), 128)
        inv = invert(amat[at, at])
        c = amat[:, at]
        r = dot_full(inv, amat[at, :])
        amat[...] -= dot_full(c, r)
        amat[:, at] = -dot_full(c, inv)
        amat[at, :] = r
        amat[at, at] = inv

    def gp_multiply(i):
        rows = pl.ds(pl.multiple_of(i * 64, 64), 64)
        ys, zs = i // 2, (i % 2) * 2
        g = gbuf[ys, pl.ds(zs, 2)].reshape(64, 2304)
        g_hi, g_lo = split(g)
        gpp[i % 4, i // 4] = dot3(g_hi, g_lo, p_hi[...], p_lo[...])

    gg.finish()

    @pl.loop(0, 8)
    def _(i):
        gp_multiply(i)

    cs = [links.push(gpp.at[(x + d) % 4], gpx.at[d - 1], me.xd(d)) for d in (1, 2, 3)]
    ycg.step()
    pl.loop(0, 2)(eliminate)
    yg.step2()
    for copy in cs:
        copy.wait_recv()
    gps[...] = gpp[x] + gpx[0] + (gpx[1] + gpx[2])
    gcopy = links.push(gps.at[1 - zh], gpa, me.anti())
    pl.loop(2, 3)(eliminate)
    yg.step3()
    gcopy.wait_recv()
    gp64[...] = gps[zh] + gpa[...]
    gp_hi, gp_lo = split(gp64[...])
    gyp[...] = dot3(gp_hi, gp_lo, xc_hi[...], xc_lo[...]).reshape(2, 4, 8, 512)
    copy = links.push(gyp.at[1 - k], gyd, me.sib())
    copy.wait_recv()
    gya[...] = gyp[k] + gyd[...]
    cs = [links.push(gya.at[(y + d) % 4], gyy.at[d - 1], me.yd(d)) for d in (1, 2, 3)]
    for copy in cs:
        copy.wait_recv()
    gyb[...] = gya[y] + gyy[0] + (gyy[1] + gyy[2])
    cs = [links.push(gyb, gyz.at[d - 1], me.zd(d)) for d in (1, 2, 3)]
    for copy in cs:
        copy.wait_recv()
    gyo[k, y] = gyb[...] + gyz[0] + (gyz[1] + gyz[2])
    cs = [links.push(gyo.at[k, y], gyo.at[k, y], me.yd(d)) for d in (1, 2, 3)]
    for copy in cs:
        copy.wait_recv()
    gycopy = links.push(gyo.at[k], gyo.at[k], me.sib())
    pl.loop(3, 4)(eliminate)
    yg.finish()
    out = pltpu.make_async_copy(ybuf, yr_hbm, lsem.at[1])
    out.start()
    ycg.finish()
    s_hi, s_lo = split(amat[...])

    @pl.loop(0, 4)
    def _(i):
        b_hi, b_lo = split(ycb[pl.ds(i * 2, 2)].reshape(144, 512))
        wt_ref[pl.ds(pl.multiple_of(i * 144, 144), 144), :] = dot3(b_hi, b_lo, s_hi, s_lo)

    gycopy.wait_recv()
    gy_hi, gy_lo = split(gyo[...].reshape(64, 512))
    w_hi, w_lo = split(wt_ref[...])
    proj_ref[...] = gp64[...] - dot3(gy_hi, gy_lo, w_hi, w_lo, NT)
    out.wait()
    links.finish()


def mega_call(projector, packed, grad):
    vm = lambda *shape, dtype=F32: pltpu.VMEM(shape, dtype)
    scratch = [
        vm(2304, 576), vm(2304, 576, dtype=BF16), vm(2304, 576, dtype=BF16),
        vm(8, 288, 128), vm(8, 72, 128), vm(576, 512, dtype=BF16), vm(576, 512, dtype=BF16),
        vm(4, 4, 2, 16, 2304), vm(4, 4, 2, 72, 512), vm(4, 4, 72, 512), vm(4, 4, 72, 512),
        vm(2, 2, 72, 512), vm(2, 4, 72, 512), vm(3, 72, 512),
        vm(4, 4, 2, 72, 512), vm(8, 72, 512), vm(72, 512),
        vm(2, 4, 4, 8, 640), vm(4, 4, 8, 640), vm(4, 4, 8, 640), vm(3, 4, 8, 640),
        vm(4, 8, 640), vm(3, 8, 640), vm(2, 8, 640), vm(4, 8, 640), vm(2, 4, 4, 8, 640), vm(512, 512),
        vm(4, 2, 64, 576), vm(3, 2, 64, 576), vm(2, 64, 576), vm(64, 576), vm(64, 576),
        vm(2, 4, 8, 512), vm(4, 8, 512), vm(4, 8, 512), vm(3, 8, 512), vm(8, 512), vm(3, 8, 512), vm(2, 4, 8, 512),
        pltpu.SemaphoreType.DMA((NSEM,)), pltpu.SemaphoreType.DMA((NSEM,)), pltpu.SemaphoreType.DMA((2,)),
    ]
    anyspace = pl.BlockSpec(memory_space=pl.ANY)
    vmem = pl.BlockSpec(memory_space=pltpu.VMEM)
    return pl.pallas_call(
        mega,
        out_shape=[
            jax.ShapeDtypeStruct((4, 4, 2, 72, 512), F32),
            jax.ShapeDtypeStruct((576, 512), F32),
            jax.ShapeDtypeStruct((64, 576), F32),
        ],
        in_specs=[anyspace, vmem, vmem],
        out_specs=[anyspace, vmem, vmem],
        scratch_shapes=scratch,
        compiler_params=pltpu.CompilerParams(
            collective_id=0, has_side_effects=True, vmem_limit_bytes=58 * 1024 * 1024),
        name="solve",
    )(projector, packed, grad)


def update_kernel(p_ref, y_ref, wt_ref, o_ref, w_hi, w_lo):
    @pl.when(pl.program_id(0) == 0)
    def _():
        w_hi[...], w_lo[...] = split(wt_ref[...])

    y_hi, y_lo = split(y_ref[...])
    o_ref[...] = p_ref[...] - dot3(y_hi, y_lo, w_hi[...], w_lo[...], NT)


def update_call(projector, y_rows, wt):
    block = 256
    return pl.pallas_call(
        update_kernel,
        grid=(2304 // block,),
        out_shape=jax.ShapeDtypeStruct((2304, 576), F32),
        in_specs=[
            pl.BlockSpec((block, 576), lambda i: (i, 0)),
            pl.BlockSpec((block, 512), lambda i: (i, 0)),
            pl.BlockSpec((576, 512), lambda i: (0, 0)),
        ],
        out_specs=pl.BlockSpec((block, 576), lambda i: (i, 0)),
        scratch_shapes=[pltpu.VMEM((576, 512), BF16), pltpu.VMEM((576, 512), BF16)],
        compiler_params=pltpu.CompilerParams(vmem_limit_bytes=32 * 1024 * 1024),
        name="update",
    )(projector, y_rows, wt)


def local(projector, saved, grad_slab):
    packed = jnp.concatenate([saved[:288], saved[288:]], axis=1)
    y_rows, wt, projected = mega_call(projector, packed, grad_slab)
    updated = update_call(projector, y_rows.reshape(2304, 512), wt)
    return (updated, projected)


def solution(mesh):
    return jax.shard_map(
        local,
        mesh=mesh,
        in_specs=(P("row", "col"), P("col", "row"), P("col", "row")),
        out_specs=(P("row", "col"), P("row", "col")),
        check_vma=False,
    )
```

time: 1080 us -> 255 us (0.24)
  waiting for transfers between devices: 839 us -> 0 us
  Pallas kernels: 0 us -> 230 us
  other arithmetic: 133 us -> 0.78 us
  matrix products: 64.1 us -> 0 us
  between operations: 17.5 us -> 0.7 us
    psum x3 -> x0, waiting for transfers between devices: 681 us -> none  [the longest x1 292 us: local(): y_rows = lax.psum(partial_value, 'col')]
    pallas_call x0 -> x2, Pallas kernels: none -> 230 us  [the longest x1 223 us: mega_call(): pl.pallas_call(mega, out_shape=[jax.ShapeDtypeStruct((4, 4, 2, 72, 512),...]
    another operation x17 -> x0, other arithmetic: 129 us -> none  [the longest x14 87.2 us: local(): factor = jnp.linalg.cholesky(system)]
    unnamed x7 -> x0, waiting for transfers between devices: 87.6 us -> none
    all_gather x2 -> x0, waiting for transfers between devices: 70.6 us -> none  [the longest x1 70.6 us: local(): saved_cols = lax.all_gather(saved, 'row', axis=1, tiled=True)]
    dot_general x4 -> x0, matrix products: 52 us -> none  [the longest x1 22.2 us: local(): jnp.dot(projector, saved_cols, precision=highest, preferred_element_type=...]
    unnamed x17 -> x15, local copies, waits for them, and re-layouts: 2.4 us -> 19.7 us
    another operation x17 -> x0, local copies, waits for them, and re-layouts: 13.7 us -> none
  transfers between devices with their start and end apart: 6 -> 0, of which waited for: 5 -> 0; matrix products, arithmetic and copies ran while one was open for 16% -> 0% of each run, Pallas kernels for 0% -> 0%
where the time goes in v1:
time: 255 us; the launch traced here: 252 us
  Pallas kernels  230 us (90%)
  local copies, waits for them, and re-layouts  20.8 us (8%)
    pallas_call x1, Pallas kernels, mega_call(): pl.pallas_call(mega, out_shape=[jax.ShapeDtypeStruct((4, 4, 2, 72, 512),...  223 us
    unnamed x15, local copies, waits for them, and re-layouts  19.7 us
    pallas_call x1, Pallas kernels, update_call(): pl.pallas_call(update_kernel, grid=(2304 // block,), out_shape=jax.ShapeD...  7.19 us

profile of v1, /device:TPU:1, one launch (start us, length us, event | category | flops | bytes accessed | tf_op | source)
XLA Modules:
  0.0 252.4 jit_solution(8706386601523732691)
XLA Ops:
  0.6 1.1 fusion
  1.7 0.1 copy.10
  1.8 0.1 copy.11
  1.9 0.8 pad_maximum_fusion.xp_ref
  2.7 6.4 %copy.8.p_hbm.p_ref = f32[2304,576]{1,0:T(8,128)} copy(f32[2304,576]{0,1:T(8,128)} %param.3) | data formatting | bytes 10616832 | tf_op args[0]
  9.1 0.0 copy-start
  9.1 223.0 %solve.1 = (f32[4,4,2,72,512]{4,3,2,1,0:T(8,128)}, f32[576,512]{1,0:T(8,128)}, f32[64,576]{1,0:T(8,128)}) custom-call(f32[2304,576]{1,0:T(8,128)} %copy.8.p_hbm.p_ref, f32[288,128]{1,0:T(8,128)} %pad_maximum_fusion.xp_ref, f32[16,2304]{1,0:T(8,128)} %g_ref.1), custom_call_target="tpu_custom_call" | custom-call | tf_op jit(solution)/shard_map/solve/pallas_call | solution.py:452
  232.0 0.0 copy-done
  232.1 0.0 copy-start.2
  232.1 2.3 copy-done.2
  234.4 0.0 copy-start.3
  234.4 1.3 copy-done.3
  235.7 7.2 %update.1 = f32[2304,576]{1,0:T(8,128)S(1)} custom-call(f32[2304,576]{1,0:T(8,128)S(1)} %copy-done, f32[2304,512]{1,0:T(8,128)S(1)} %bitcast.1, f32[576,512]{1,0:T(8,128)S(1)} %copy-done.3), custom_call_target="tpu_custom_call" | custom-call | tf_op jit(solution)/shard_map/update/pallas_call | solution.py:479
  242.9 0.0 copy-start.1
  242.9 2.5 %copy-done.1 = f32[2304,576]{1,0:T(8,128)} copy-done((f32[2304,576]{1,0:T(8,128)}, f32[2304,576]{1,0:T(8,128)S(1)}, u32[]{:S(2)}) %copy-start.1) | copy-done | bytes 5308440
  245.4 0.0 copy-start.4
  245.4 6.3 %copy.9 = f32[2304,576]{0,1:T(8,128)} copy(f32[2304,576]{1,0:T(8,128)} %copy-done.1) | data formatting | bytes 10616832
  251.8 0.0 copy-done.4
  251.8 0.7 copy.13
Async XLA Ops:
  9.1 223.0 %copy-start = (f32[2304,576]{1,0:T(8,128)S(1)}, f32[2304,576]{1,0:T(8,128)}, u32[]{:S(2)}) copy-start(f32[2304,576]{1,0:T(8,128)} %copy.8.p_hbm.p_ref) | copy-start | bytes 15925252
  232.1 2.3 copy-start.2
  234.4 1.3 copy-start.3
  242.9 2.5 %copy-start.1 = (f32[2304,576]{1,0:T(8,128)}, f32[2304,576]{1,0:T(8,128)S(1)}, u32[]{:S(2)}) copy-start(f32[2304,576]{1,0:T(8,128)S(1)} %update.1) | copy-start | bytes 15925252
  245.4 6.4 %copy-start.4 = (f32[64,576]{1,0:T(8,128)S(1)}, f32[64,576]{1,0:T(8,128)}, u32[]{:S(2)}) copy-start(f32[64,576]{1,0:T(8,128)} %get-tuple-element.15) | copy-start | bytes 442372

commit v2 on v1

--- a/solution.py
+++ b/solution.py
@@ -199,21 +199,48 @@
         pl.when(jnp.logical_not(self.here))(lambda: self.remote.wait_send())
 
 
+def lanes(v, j):
+    return jnp.broadcast_to(v[:, j:j + 1], (8, 128))
+
+
+def rows8(v, i):
+    return jnp.broadcast_to(v[i:i + 1, :], (8, 128))
+
+
+def total(terms):
+    while len(terms) > 1:
+        terms = [a + b for a, b in zip(terms[::2], terms[1::2])]
+    return terms[0]
+
+
 def invert(a):
-    n = a.shape[0]
-    ri = lax.broadcasted_iota(jnp.int32, (n, n), 0)
-    ci = lax.broadcasted_iota(jnp.int32, (n, n), 1)
-    for k in range(n):
-        row = a[k:k + 1, :]
-        col = a[:, k:k + 1]
-        p = 1.0 / a[k:k + 1, k:k + 1]
-        rp = row * p
-        b = jnp.where(ci == k, -(col * p), a - col * rp)
-        a = jnp.where(ri == k, jnp.where(ci[0:1] == k, p, rp), b)
-    return a
-
-
-def mega(p_hbm, xp_ref, g_ref, yr_hbm, wt_ref, proj_ref,
+    s = lax.broadcasted_iota(jnp.int32, (8, 128), 0)
+    lane = lax.broadcasted_iota(jnp.int32, (8, 128), 1)
+    tiles = [a[8 * i:8 * i + 8, :] for i in range(16)]
+    for g in range(16):
+        e = [lanes(tiles[g], 8 * g + j) for j in range(8)]
+        for i in range(8):
+            p = 1.0 / rows8(e[i], i)
+            new = []
+            for j in range(8):
+                if j == i:
+                    new.append(jnp.where(s == i, p, -(e[i] * p)))
+                else:
+                    r = rows8(e[j], i) * p
+                    new.append(jnp.where(s == i, r, e[j] - e[i] * r))
+            e = new
+        inside = jnp.logical_and(lane >= 8 * g, lane < 8 * g + 8)
+        unit = jnp.where(inside, jnp.where(lane - 8 * g == s, 1.0, 0.0), tiles[g])
+        pivot = total([e[j] * rows8(unit, j) for j in range(8)])
+        each = [rows8(pivot, j) for j in range(8)]
+        tiles = [
+            pivot if i == g else jnp.where(inside, 0.0, t) - total([lanes(t, 8 * g + j) * each[j] for j in range(8)])
+            for i, t in enumerate(tiles)
+        ]
+    return jnp.concatenate(tiles, axis=0)
+
+
+def mega(p_hbm, xt_ref, g_ref, yr_hbm, wt_ref, proj_ref,
          pst, p_hi, p_lo, xbuf, xs, xc_hi, xc_lo, gbuf, part, d2d, csum, r1, r2, rz, ybuf, ycb, x72,
          gram, gram_in, ga, gy_in, gb, gx_in, gc, gz_in, gout, amat, gpp, gpx, gps, gpa, gp64,
          gyp, gyd, gya, gyy, gyb, gyz, gyo, send, recv, lsem):
@@ -222,27 +249,28 @@
     links = Links(me, send, recv)
     pcopy = pltpu.make_async_copy(p_hbm, pst, lsem.at[0])
     pcopy.start()
-    xbuf[row] = xp_ref[...]
+    xp_ref = xbuf.at[row]
+    xp_ref[...] = jnp.concatenate([xt_ref[:, 0:288], xt_ref[:, 288:576]], axis=0).T
     gbuf[y, zl, k] = g_ref[...]
     barrier(me)
     xg = RowGather(links, xbuf)
     xg.start()
-    base_s, base_r = links.slot(8), links.slot(8)
-    for q in range(8):
-        LooseCopy(links, xp_ref.at[pl.ds(72 * (q % 4), 72)], xs.at[row], me.strip(q), base_s + q, base_r + row)
     gg = PlaneGather(links, gbuf)
     gg.start()
     pcopy.wait()
 
-    @pl.loop(0, 36)
+    @pl.loop(0, 18)
     def _(i):
-        rows = pl.ds(pl.multiple_of(i * 64, 64), 64)
-        p_hi[rows], p_lo[rows] = split(pst[rows])
+        rows = pl.ds(pl.multiple_of(i * 128, 128), 128)
+        p_hi[rows], p_lo[rows] = split(pst[:, rows].T)
 
     xg.step()
     gg.step1()
     lane = lax.broadcasted_iota(jnp.int32, (288, 128), 1)
     xg.finish()
+    base_s, base_r = links.slot(8), links.slot(8)
+    for q in range(8):
+        LooseCopy(links, xp_ref.at[pl.ds(72 * (q % 4), 72)], xs.at[row], me.strip(q), base_s + q, base_r + row)
     for m in range(4):
         b0, b1 = xbuf[2 * m], xbuf[2 * m + 1]
         cols = pl.ds(128 * m, 128)
@@ -250,10 +278,11 @@
         xc_hi[288:576, cols], xc_lo[288:576, cols] = split(jnp.where(lane < 64, pltpu.roll(b0, 64, 1), b1))
 
     def multiply(ay):
-        @pl.loop(0, 4)
+        @pl.loop(0, 2)
         def _(z):
-            rows = pl.ds(pl.multiple_of(ay * 576 + z * 144, 144), 144)
-            part[ay, z] = dot3(p_hi[rows], p_lo[rows], xc_hi[...], xc_lo[...]).reshape(2, 72, 512)
+            rows = pl.ds(pl.multiple_of(ay * 576 + z * 288, 288), 288)
+            part[ay, pl.ds(z * 2, 2)] = dot3(p_hi[rows], p_lo[rows], xc_hi[...], xc_lo[...]).reshape(2, 2, 72, 512)
+
         return links.push(part.at[ay, :, 1 - k], d2d.at[ay], me.sib())
 
     def add_pair(ay, copy):
@@ -282,10 +311,27 @@
         csum[y3, z + 2] += r1[1, z]
     down2 = links.push(csum.at[y3], r2.at[1], me.yd(3))
     add_pair(y, c0)
+    gg.step2()
+
+    def gp_multiply(i):
+        g_hi, g_lo = split(gbuf[pl.ds(2 * i, 2)].reshape(256, 2304))
+        gpp[:, i] = dot3(g_hi, g_lo, p_hi[...], p_lo[...]).reshape(4, 64, 576)
+
+    gg.step3()
+    gg.finish()
+    pl.loop(0, 2)(gp_multiply)
+    gpc = [links.push(gpp.at[(x + d) % 4], gpx.at[d - 1], me.xd(d)) for d in (1, 2, 3)]
+    up2.wait_recv()
+    down2.wait_recv()
+
+    @pl.loop(0, 4)
+    def _(z):
+        csum[y, z] = csum[y, z] + (r2[0, z] + r2[1, z])
+
+    zc = [links.push(csum.at[y, (zl + d) % 4], rz.at[d - 1], me.zd(d)) for d in (1, 2, 3)]
 
     for r in range(8):
-        links_recv = pltpu.make_async_copy(xs.at[r], xs.at[r], recv.at[base_r + r])
-        links_recv.wait()
+        pltpu.make_async_copy(xs.at[r], xs.at[r], recv.at[base_r + r]).wait()
     lane72 = lax.broadcasted_iota(jnp.int32, (72, 128), 1)
     flip = (col % 8) >= 4
     for m in range(4):
@@ -293,26 +339,13 @@
         first = jnp.where(lane72 < 64, b0, pltpu.roll(b1, 64, 1))
         second = jnp.where(lane72 < 64, pltpu.roll(b0, 64, 1), b1)
         x72[:, 128 * m:128 * m + 128] = jnp.where(flip, second, first)
-
-    gg.step2()
-    up2.wait_recv()
-    down2.wait_recv()
-
-    @pl.loop(0, 4)
-    def _(z):
-        csum[y, z] = csum[y, z] + (r2[0, z] + r2[1, z])
-
-    zc = []
-    for d in (1, 2, 3):
-        zc.append(links.push(csum.at[y, (zl + d) % 4], rz.at[d - 1], me.zd(d)))
-    gg.step3()
     for copy in zc:
         copy.wait_recv()
-    y72 = csum[y, zl] + rz[0] + (rz[1] + rz[2])
-    ybuf[y, zl, k] = y72
-    yg = PlaneGather(links, ybuf)
-    yg.start()
-    yc = LooseCopy(links, ybuf.at[y, zl, k], ycb.at[col % 8], me.strip_source(col % 8), links.slot(), links.slot())
+    ybuf[y, zl, k] = csum[y, zl] + rz[0] + (rz[1] + rz[2])
+    for copy in gpc:
+        copy.wait_recv()
+    gps[...] = gpp[x] + gpx[0] + (gpx[1] + gpx[2])
+    gcopy = links.push(gps.at[1 - zh], gpa, me.anti())
 
     yv = ybuf[y, zl, k]
     for i, (top, left) in enumerate(((0, 0), (128, 0), (128, 256), (0, 128))):
@@ -323,31 +356,50 @@
     for i in range(4):
         ga[i] = gram[k, i] + gram_in[i]
     cs = [links.push(ga.at[(y + d) % 4], gy_in.at[d - 1], me.yd(d)) for d in (1, 2, 3)]
+    gcopy.wait_recv()
+    gp64[...] = gps[zh] + gpa[...]
+    gp_hi, gp_lo = split(gp64[...])
+    gyp[...] = dot3(gp_hi, gp_lo, xc_hi[...], xc_lo[...]).reshape(2, 4, 8, 512)
+    ycopy = links.push(gyp.at[1 - k], gyd, me.sib())
     for copy in cs:
         copy.wait_recv()
     gb[...] = ga[y] + gy_in[0] + (gy_in[1] + gy_in[2])
     cs = [links.push(gb.at[(x + d) % 4], gx_in.at[d - 1], me.xd(d)) for d in (1, 2, 3)]
+    ycopy.wait_recv()
+    gya[...] = gyp[k] + gyd[...]
+    ys = [links.push(gya.at[(y + d) % 4], gyy.at[d - 1], me.yd(d)) for d in (1, 2, 3)]
     for copy in cs:
         copy.wait_recv()
     gc[0] = gb[x] + gx_in[0] + (gx_in[1] + gx_in[2])
     cs = [links.push(gc.at[0], gz_in.at[d - 1], me.zd(d)) for d in (1, 2, 3)]
+    for copy in ys:
+        copy.wait_recv()
+    gyb[...] = gya[y] + gyy[0] + (gyy[1] + gyy[2])
+    ys = [links.push(gyb, gyz.at[d - 1], me.zd(d)) for d in (1, 2, 3)]
     for copy in cs:
         copy.wait_recv()
     gc[1] = gc[0] + gz_in[0] + (gz_in[1] + gz_in[2])
     copy = links.push(gc.at[1], gz_in.at[3], me.anti())
+    for c in ys:
+        c.wait_recv()
+    gyo[k, y] = gyb[...] + gyz[0] + (gyz[1] + gyz[2])
+    ys = [links.push(gyo.at[k, y], gyo.at[k, y], me.yd(d)) for d in (1, 2, 3)]
     copy.wait_recv()
     gout[k, y, x] = gc[1] + gz_in[3]
     cs = [links.push(gout.at[k, y, x], gout.at[k, y, x], me.xd(d)) for d in (1, 2, 3)]
+    yg = PlaneGather(links, ybuf)
+    yg.start()
     for copy in cs:
         copy.wait_recv()
     cs = [links.push(gout.at[k, y], gout.at[k, y], me.yd(d)) for d in (1, 2, 3)]
+    for copy in ys:
+        copy.wait_recv()
+    ycopy = links.push(gyo.at[k], gyo.at[k], me.sib())
     for copy in cs:
         copy.wait_recv()
     copy = links.push(gout.at[k], gout.at[k], me.sib())
-    yg.step1()
-    yc.remote.wait_recv()
-    ycg = RowGather(links, ycb)
-    ycg.start()
+    yc = LooseCopy(links, ybuf.at[y, zl, k], ycb.at[col % 8], me.strip_source(col % 8), links.slot(), links.slot())
+    ycopy.wait_recv()
     copy.wait_recv()
 
     ri = lax.broadcasted_iota(jnp.int32, (128, 128), 0)
@@ -371,48 +423,16 @@
         amat[at, :] = r
         amat[at, at] = inv
 
-    def gp_multiply(i):
-        rows = pl.ds(pl.multiple_of(i * 64, 64), 64)
-        ys, zs = i // 2, (i % 2) * 2
-        g = gbuf[ys, pl.ds(zs, 2)].reshape(64, 2304)
-        g_hi, g_lo = split(g)
-        gpp[i % 4, i // 4] = dot3(g_hi, g_lo, p_hi[...], p_lo[...])
-
-    gg.finish()
-
-    @pl.loop(0, 8)
-    def _(i):
-        gp_multiply(i)
-
-    cs = [links.push(gpp.at[(x + d) % 4], gpx.at[d - 1], me.xd(d)) for d in (1, 2, 3)]
+    pl.loop(0, 1)(eliminate)
+    yg.step1()
+    yc.remote.wait_recv()
+    ycg = RowGather(links, ycb)
+    ycg.start()
+    pl.loop(1, 2)(eliminate)
+    yg.step2()
     ycg.step()
-    pl.loop(0, 2)(eliminate)
-    yg.step2()
-    for copy in cs:
-        copy.wait_recv()
-    gps[...] = gpp[x] + gpx[0] + (gpx[1] + gpx[2])
-    gcopy = links.push(gps.at[1 - zh], gpa, me.anti())
     pl.loop(2, 3)(eliminate)
     yg.step3()
-    gcopy.wait_recv()
-    gp64[...] = gps[zh] + gpa[...]
-    gp_hi, gp_lo = split(gp64[...])
-    gyp[...] = dot3(gp_hi, gp_lo, xc_hi[...], xc_lo[...]).reshape(2, 4, 8, 512)
-    copy = links.push(gyp.at[1 - k], gyd, me.sib())
-    copy.wait_recv()
-    gya[...] = gyp[k] + gyd[...]
-    cs = [links.push(gya.at[(y + d) % 4], gyy.at[d - 1], me.yd(d)) for d in (1, 2, 3)]
-    for copy in cs:
-        copy.wait_recv()
-    gyb[...] = gya[y] + gyy[0] + (gyy[1] + gyy[2])
-    cs = [links.push(gyb, gyz.at[d - 1], me.zd(d)) for d in (1, 2, 3)]
-    for copy in cs:
-        copy.wait_recv()
-    gyo[k, y] = gyb[...] + gyz[0] + (gyz[1] + gyz[2])
-    cs = [links.push(gyo.at[k, y], gyo.at[k, y], me.yd(d)) for d in (1, 2, 3)]
-    for copy in cs:
-        copy.wait_recv()
-    gycopy = links.push(gyo.at[k], gyo.at[k], me.sib())
     pl.loop(3, 4)(eliminate)
     yg.finish()
     out = pltpu.make_async_copy(ybuf, yr_hbm, lsem.at[1])
@@ -420,12 +440,11 @@
     ycg.finish()
     s_hi, s_lo = split(amat[...])
 
-    @pl.loop(0, 4)
+    @pl.loop(0, 2)
     def _(i):
-        b_hi, b_lo = split(ycb[pl.ds(i * 2, 2)].reshape(144, 512))
-        wt_ref[pl.ds(pl.multiple_of(i * 144, 144), 144), :] = dot3(b_hi, b_lo, s_hi, s_lo)
-
-    gycopy.wait_recv()
+        b_hi, b_lo = split(ycb[pl.ds(i * 4, 4)].reshape(288, 512))
+        wt_ref[pl.ds(pl.multiple_of(i * 288, 288), 288), :] = dot3(b_hi, b_lo, s_hi, s_lo)
+
     gy_hi, gy_lo = split(gyo[...].reshape(64, 512))
     w_hi, w_lo = split(wt_ref[...])
     proj_ref[...] = gp64[...] - dot3(gy_hi, gy_lo, w_hi, w_lo, NT)
@@ -433,10 +452,10 @@
     links.finish()
 
 
-def mega_call(projector, packed, grad):
+def mega_call(projector, saved, grad):
     vm = lambda *shape, dtype=F32: pltpu.VMEM(shape, dtype)
     scratch = [
-        vm(2304, 576), vm(2304, 576, dtype=BF16), vm(2304, 576, dtype=BF16),
+        vm(576, 2304), vm(2304, 576, dtype=BF16), vm(2304, 576, dtype=BF16),
         vm(8, 288, 128), vm(8, 72, 128), vm(576, 512, dtype=BF16), vm(576, 512, dtype=BF16),
         vm(4, 4, 2, 16, 2304), vm(4, 4, 2, 72, 512), vm(4, 4, 72, 512), vm(4, 4, 72, 512),
         vm(2, 2, 72, 512), vm(2, 4, 72, 512), vm(3, 72, 512),
@@ -462,7 +481,7 @@
         compiler_params=pltpu.CompilerParams(
             collective_id=0, has_side_effects=True, vmem_limit_bytes=58 * 1024 * 1024),
         name="solve",
-    )(projector, packed, grad)
+    )(projector, saved, grad)
 
 
 def update_kernel(p_ref, y_ref, wt_ref, o_ref, w_hi, w_lo):
@@ -471,7 +490,7 @@
         w_hi[...], w_lo[...] = split(wt_ref[...])
 
     y_hi, y_lo = split(y_ref[...])
-    o_ref[...] = p_ref[...] - dot3(y_hi, y_lo, w_hi[...], w_lo[...], NT)
+    o_ref[...] = p_ref[...] - dot3(w_hi[...], w_lo[...], y_hi, y_lo, NT)
 
 
 def update_call(projector, y_rows, wt):
@@ -479,24 +498,24 @@
     return pl.pallas_call(
         update_kernel,
         grid=(2304 // block,),
-        out_shape=jax.ShapeDtypeStruct((2304, 576), F32),
+        out_shape=jax.ShapeDtypeStruct((576, 2304), F32),
         in_specs=[
-            pl.BlockSpec((block, 576), lambda i: (i, 0)),
+            pl.BlockSpec((576, block), lambda i: (0, i)),
             pl.BlockSpec((block, 512), lambda i: (i, 0)),
             pl.BlockSpec((576, 512), lambda i: (0, 0)),
         ],
-        out_specs=pl.BlockSpec((block, 576), lambda i: (i, 0)),
+        out_specs=pl.BlockSpec((576, block), lambda i: (0, i)),
         scratch_shapes=[pltpu.VMEM((576, 512), BF16), pltpu.VMEM((576, 512), BF16)],
-        compiler_params=pltpu.CompilerParams(vmem_limit_bytes=32 * 1024 * 1024),
+        compiler_params=pltpu.CompilerParams(vmem_limit_bytes=58 * 1024 * 1024),
         name="update",
     )(projector, y_rows, wt)
 
 
 def local(projector, saved, grad_slab):
-    packed = jnp.concatenate([saved[:288], saved[288:]], axis=1)
-    y_rows, wt, projected = mega_call(projector, packed, grad_slab)
-    updated = update_call(projector, y_rows.reshape(2304, 512), wt)
-    return (updated, projected)
+    turned = projector.T
+    y_rows, wt, projected = mega_call(turned, saved.T, grad_slab)
+    updated = update_call(turned, y_rows.reshape(2304, 512), wt)
+    return (updated.T, projected)
 
 
 def solution(mesh):

time: 255 us -> 204 us (0.80)
  Pallas kernels: 230 us -> 203 us
  local copies, waits for them, and re-layouts: 20.8 us -> 0.67 us
    pallas_call x1, Pallas kernels: 223 us -> 191 us  [mega_call(): pl.pallas_call(mega, out_shape=[jax.ShapeDtypeStruct((4, 4, 2, 72, 512),...]
    unnamed x15 -> x3, local copies, waits for them, and re-layouts: 19.7 us -> 0.67 us
    pallas_call x1, Pallas kernels: 7.19 us -> 11.9 us  [update_call(): pl.pallas_call(update_kernel, grid=(2304 // block,), out_shape=jax.ShapeD...]
where the time goes in v2:
time: 204 us
  Pallas kernels  203 us (100%)
    pallas_call x1, Pallas kernels, mega_call(): pl.pallas_call(mega, out_shape=[jax.ShapeDtypeStruct((4, 4, 2, 72, 512),...  191 us
    pallas_call x1, Pallas kernels, update_call(): pl.pallas_call(update_kernel, grid=(2304 // block,), out_shape=jax.ShapeD...  11.9 us

profile of v2, /device:TPU:1, one launch (start us, length us, event | category | flops | bytes accessed | tf_op | source)
XLA Modules:
  0.0 203.9 jit_solution(14472852472969872485)
XLA Ops:
  0.6 190.7 %solve.1 = (f32[4,4,2,72,512]{4,3,2,1,0:T(8,128)}, f32[576,512]{1,0:T(8,128)}, f32[64,576]{1,0:T(8,128)}) custom-call(f32[576,2304]{1,0:T(8,128)} %bitcast.4, f32[64,576]{1,0:T(8,128)} %bitcast.8, f32[16,2304]{1,0:T(8,128)} %g_ref.1), custom_call_target="tpu_custom_call" | custom-call | tf_op jit(solution)/shard_map/solve/pallas_call | solution.py:471
  191.3 0.0 copy-start
  191.3 11.9 %update.1 = f32[576,2304]{1,0:T(8,128)} custom-call(f32[576,2304]{1,0:T(8,128)} %bitcast.5, f32[2304,512]{1,0:T(8,128)} %bitcast.7, f32[576,512]{1,0:T(8,128)} %get-tuple-element.6.wt_ref), custom_call_target="tpu_custom_call" | custom-call | tf_op jit(solution)/shard_map/update/pallas_call | solution.py:498
  203.2 0.0 copy-done
  203.2 0.7 copy.6
Async XLA Ops:
  191.3 11.9 %copy-start = (f32[64,576]{1,0:T(8,128)S(1)}, f32[64,576]{1,0:T(8,128)}, u32[]{:S(2)}) copy-start(f32[64,576]{1,0:T(8,128)} %get-tuple-element.11) | copy-start | bytes 442372

commit v3 on v2

--- a/solution.py
+++ b/solution.py
@@ -110,7 +110,9 @@
 
     def pair(self, y):
         part = self.buf.at[y, :, self.me.k]
-        self.pairs.append(self.links.push(part, part, self.me.sib()))
+        copy = self.links.push(part, part, self.me.sib())
+        self.pairs.append(copy)
+        return copy
 
     def step1(self):
         me, buf = self.me, self.buf
@@ -120,7 +122,7 @@
         mine = buf.at[me.y, :, me.k]
         self.up = self.links.push(mine, mine, me.yd(1))
         self.down = self.links.push(mine, mine, me.yd(3))
-        self.pair(me.y)
+        self.own = self.pair(me.y)
 
     def step2(self):
         me, buf = self.me, self.buf
@@ -131,13 +133,13 @@
         self.down.wait_recv()
         half = buf.at[above, pl.ds(2, 2), me.k]
         self.down2 = self.links.push(half, half, me.yd(3))
-        self.pair(below)
-        self.pair(above)
+        self.below = self.pair(below)
+        self.above = self.pair(above)
 
     def step3(self):
         self.up2.wait_recv()
         self.down2.wait_recv()
-        self.pair((self.me.y + 2) % 4)
+        self.last = self.pair((self.me.y + 2) % 4)
 
     def finish(self):
         for copy in self.pairs:
@@ -256,7 +258,6 @@
     xg = RowGather(links, xbuf)
     xg.start()
     gg = PlaneGather(links, gbuf)
-    gg.start()
     pcopy.wait()
 
     @pl.loop(0, 18)
@@ -265,7 +266,7 @@
         p_hi[rows], p_lo[rows] = split(pst[:, rows].T)
 
     xg.step()
-    gg.step1()
+    gg.start()
     lane = lax.broadcasted_iota(jnp.int32, (288, 128), 1)
     xg.finish()
     base_s, base_r = links.slot(8), links.slot(8)
@@ -311,16 +312,12 @@
         csum[y3, z + 2] += r1[1, z]
     down2 = links.push(csum.at[y3], r2.at[1], me.yd(3))
     add_pair(y, c0)
-    gg.step2()
-
-    def gp_multiply(i):
-        g_hi, g_lo = split(gbuf[pl.ds(2 * i, 2)].reshape(256, 2304))
-        gpp[:, i] = dot3(g_hi, g_lo, p_hi[...], p_lo[...]).reshape(4, 64, 576)
-
-    gg.step3()
-    gg.finish()
-    pl.loop(0, 2)(gp_multiply)
-    gpc = [links.push(gpp.at[(x + d) % 4], gpx.at[d - 1], me.xd(d)) for d in (1, 2, 3)]
+
+    def gp_multiply(ay, copy):
+        copy.wait_recv()
+        g_hi, g_lo = split(gbuf[ay].reshape(128, 2304))
+        gpp[pl.ds(2 * (ay % 2), 2), ay // 2] = dot3(g_hi, g_lo, p_hi[...], p_lo[...]).reshape(2, 64, 576)
+
     up2.wait_recv()
     down2.wait_recv()
 
@@ -329,6 +326,7 @@
         csum[y, z] = csum[y, z] + (r2[0, z] + r2[1, z])
 
     zc = [links.push(csum.at[y, (zl + d) % 4], rz.at[d - 1], me.zd(d)) for d in (1, 2, 3)]
+    gg.step1()
 
     for r in range(8):
         pltpu.make_async_copy(xs.at[r], xs.at[r], recv.at[base_r + r]).wait()
@@ -339,13 +337,10 @@
         first = jnp.where(lane72 < 64, b0, pltpu.roll(b1, 64, 1))
         second = jnp.where(lane72 < 64, pltpu.roll(b0, 64, 1), b1)
         x72[:, 128 * m:128 * m + 128] = jnp.where(flip, second, first)
+    gp_multiply(y, gg.own)
     for copy in zc:
         copy.wait_recv()
     ybuf[y, zl, k] = csum[y, zl] + rz[0] + (rz[1] + rz[2])
-    for copy in gpc:
-        copy.wait_recv()
-    gps[...] = gpp[x] + gpx[0] + (gpx[1] + gpx[2])
-    gcopy = links.push(gps.at[1 - zh], gpa, me.anti())
 
     yv = ybuf[y, zl, k]
     for i, (top, left) in enumerate(((0, 0), (128, 0), (128, 256), (0, 128))):
@@ -356,50 +351,37 @@
     for i in range(4):
         ga[i] = gram[k, i] + gram_in[i]
     cs = [links.push(ga.at[(y + d) % 4], gy_in.at[d - 1], me.yd(d)) for d in (1, 2, 3)]
-    gcopy.wait_recv()
-    gp64[...] = gps[zh] + gpa[...]
-    gp_hi, gp_lo = split(gp64[...])
-    gyp[...] = dot3(gp_hi, gp_lo, xc_hi[...], xc_lo[...]).reshape(2, 4, 8, 512)
-    ycopy = links.push(gyp.at[1 - k], gyd, me.sib())
     for copy in cs:
         copy.wait_recv()
     gb[...] = ga[y] + gy_in[0] + (gy_in[1] + gy_in[2])
     cs = [links.push(gb.at[(x + d) % 4], gx_in.at[d - 1], me.xd(d)) for d in (1, 2, 3)]
-    ycopy.wait_recv()
-    gya[...] = gyp[k] + gyd[...]
-    ys = [links.push(gya.at[(y + d) % 4], gyy.at[d - 1], me.yd(d)) for d in (1, 2, 3)]
+    gg.step2()
     for copy in cs:
         copy.wait_recv()
     gc[0] = gb[x] + gx_in[0] + (gx_in[1] + gx_in[2])
     cs = [links.push(gc.at[0], gz_in.at[d - 1], me.zd(d)) for d in (1, 2, 3)]
-    for copy in ys:
-        copy.wait_recv()
-    gyb[...] = gya[y] + gyy[0] + (gyy[1] + gyy[2])
-    ys = [links.push(gyb, gyz.at[d - 1], me.zd(d)) for d in (1, 2, 3)]
+    gp_multiply((y + 1) % 4, gg.above)
     for copy in cs:
         copy.wait_recv()
     gc[1] = gc[0] + gz_in[0] + (gz_in[1] + gz_in[2])
     copy = links.push(gc.at[1], gz_in.at[3], me.anti())
-    for c in ys:
-        c.wait_recv()
-    gyo[k, y] = gyb[...] + gyz[0] + (gyz[1] + gyz[2])
-    ys = [links.push(gyo.at[k, y], gyo.at[k, y], me.yd(d)) for d in (1, 2, 3)]
+    gg.step3()
     copy.wait_recv()
     gout[k, y, x] = gc[1] + gz_in[3]
     cs = [links.push(gout.at[k, y, x], gout.at[k, y, x], me.xd(d)) for d in (1, 2, 3)]
     yg = PlaneGather(links, ybuf)
     yg.start()
+    gp_multiply((y + 3) % 4, gg.below)
     for copy in cs:
         copy.wait_recv()
     cs = [links.push(gout.at[k, y], gout.at[k, y], me.yd(d)) for d in (1, 2, 3)]
-    for copy in ys:
-        copy.wait_recv()
-    ycopy = links.push(gyo.at[k], gyo.at[k], me.sib())
+    gp_multiply((y + 2) % 4, gg.last)
     for copy in cs:
         copy.wait_recv()
     copy = links.push(gout.at[k], gout.at[k], me.sib())
     yc = LooseCopy(links, ybuf.at[y, zl, k], ycb.at[col % 8], me.strip_source(col % 8), links.slot(), links.slot())
-    ycopy.wait_recv()
+    gpc = [links.push(gpp.at[(x + d) % 4], gpx.at[d - 1], me.xd(d)) for d in (1, 2, 3)]
+    yg.step1()
     copy.wait_recv()
 
     ri = lax.broadcasted_iota(jnp.int32, (128, 128), 0)
@@ -424,19 +406,41 @@
         amat[at, at] = inv
 
     pl.loop(0, 1)(eliminate)
-    yg.step1()
     yc.remote.wait_recv()
     ycg = RowGather(links, ycb)
     ycg.start()
+    yg.step2()
+    for copy in gpc:
+        copy.wait_recv()
+    gps[...] = gpp[x] + gpx[0] + (gpx[1] + gpx[2])
+    gcopy = links.push(gps.at[1 - zh], gpa, me.anti())
     pl.loop(1, 2)(eliminate)
-    yg.step2()
     ycg.step()
+    yg.step3()
+    gcopy.wait_recv()
+    gp64[...] = gps[zh] + gpa[...]
+    gp_hi, gp_lo = split(gp64[...])
+    gyp[...] = dot3(gp_hi, gp_lo, xc_hi[...], xc_lo[...]).reshape(2, 4, 8, 512)
+    copy = links.push(gyp.at[1 - k], gyd, me.sib())
+    copy.wait_recv()
+    gya[...] = gyp[k] + gyd[...]
+    cs = [links.push(gya.at[(y + d) % 4], gyy.at[d - 1], me.yd(d)) for d in (1, 2, 3)]
     pl.loop(2, 3)(eliminate)
-    yg.step3()
-    pl.loop(3, 4)(eliminate)
+    for copy in cs:
+        copy.wait_recv()
+    gyb[...] = gya[y] + gyy[0] + (gyy[1] + gyy[2])
+    cs = [links.push(gyb, gyz.at[d - 1], me.zd(d)) for d in (1, 2, 3)]
     yg.finish()
     out = pltpu.make_async_copy(ybuf, yr_hbm, lsem.at[1])
     out.start()
+    for copy in cs:
+        copy.wait_recv()
+    gyo[k, y] = gyb[...] + gyz[0] + (gyz[1] + gyz[2])
+    cs = [links.push(gyo.at[k, y], gyo.at[k, y], me.yd(d)) for d in (1, 2, 3)]
+    pl.loop(3, 4)(eliminate)
+    for copy in cs:
+        copy.wait_recv()
+    ycopy = links.push(gyo.at[k], gyo.at[k], me.sib())
     ycg.finish()
     s_hi, s_lo = split(amat[...])
 
@@ -445,6 +449,7 @@
         b_hi, b_lo = split(ycb[pl.ds(i * 4, 4)].reshape(288, 512))
         wt_ref[pl.ds(pl.multiple_of(i * 288, 288), 288), :] = dot3(b_hi, b_lo, s_hi, s_lo)
 
+    ycopy.wait_recv()
     gy_hi, gy_lo = split(gyo[...].reshape(64, 512))
     w_hi, w_lo = split(wt_ref[...])
     proj_ref[...] = gp64[...] - dot3(gy_hi, gy_lo, w_hi, w_lo, NT)
@@ -484,17 +489,19 @@
     )(projector, saved, grad)
 
 
-def update_kernel(p_ref, y_ref, wt_ref, o_ref, w_hi, w_lo):
+def update_kernel(p_ref, y_ref, wt_ref, o_ref, w):
     @pl.when(pl.program_id(0) == 0)
     def _():
-        w_hi[...], w_lo[...] = split(wt_ref[...])
+        w_hi, w_lo = split(wt_ref[...])
+        w[...] = jnp.concatenate([w_hi, w_hi, w_lo], axis=1)
 
     y_hi, y_lo = split(y_ref[...])
-    o_ref[...] = p_ref[...] - dot3(w_hi[...], w_lo[...], y_hi, y_lo, NT)
+    y = jnp.concatenate([y_hi, y_lo, y_hi], axis=1)
+    o_ref[...] = p_ref[...] - lax.dot_general(w[...], y, NT, preferred_element_type=F32)
 
 
 def update_call(projector, y_rows, wt):
-    block = 256
+    block = 768
     return pl.pallas_call(
         update_kernel,
         grid=(2304 // block,),
@@ -505,7 +512,7 @@
             pl.BlockSpec((576, 512), lambda i: (0, 0)),
         ],
         out_specs=pl.BlockSpec((576, block), lambda i: (0, i)),
-        scratch_shapes=[pltpu.VMEM((576, 512), BF16), pltpu.VMEM((576, 512), BF16)],
+        scratch_shapes=[pltpu.VMEM((576, 1536), BF16)],
         compiler_params=pltpu.CompilerParams(vmem_limit_bytes=58 * 1024 * 1024),
         name="update",
     )(projector, y_rows, wt)

time: 204 us -> 187 us (0.917)
  Pallas kernels: 203 us -> 186 us
    pallas_call x1, Pallas kernels: 191 us -> 176 us  [mega_call(): pl.pallas_call(mega, out_shape=[jax.ShapeDtypeStruct((4, 4, 2, 72, 512),...]
    pallas_call x1, Pallas kernels: 11.9 us -> 9.57 us  [update_call(): pl.pallas_call(update_kernel, grid=(2304 // block,), out_shape=jax.ShapeD...]
where the time goes in v3:
time: 187 us
  Pallas kernels  186 us (99%)
    pallas_call x1, Pallas kernels, mega_call(): pl.pallas_call(mega, out_shape=[jax.ShapeDtypeStruct((4, 4, 2, 72, 512),...  176 us
    pallas_call x1, Pallas kernels, update_call(): pl.pallas_call(update_kernel, grid=(2304 // block,), out_shape=jax.ShapeD...  9.57 us

profile of v3, /device:TPU:1, one launch (start us, length us, event | category | flops | bytes accessed | tf_op | source)
XLA Modules:
  0.0 187.0 jit_solution(4885749891233988930)
XLA Ops:
  0.6 176.1 %solve.1 = (f32[4,4,2,72,512]{4,3,2,1,0:T(8,128)}, f32[576,512]{1,0:T(8,128)}, f32[64,576]{1,0:T(8,128)}) custom-call(f32[576,2304]{1,0:T(8,128)} %bitcast.4, f32[64,576]{1,0:T(8,128)} %bitcast.8, f32[16,2304]{1,0:T(8,128)} %g_ref.1), custom_call_target="tpu_custom_call" | custom-call | tf_op jit(solution)/shard_map/solve/pallas_call | solution.py:476
  176.8 0.0 copy-start
  176.8 9.6 %update.1 = f32[576,2304]{1,0:T(8,128)} custom-call(f32[576,2304]{1,0:T(8,128)} %bitcast.5, f32[2304,512]{1,0:T(8,128)} %bitcast.7, f32[576,512]{1,0:T(8,128)} %get-tuple-element.6.wt_ref), custom_call_target="tpu_custom_call" | custom-call | tf_op jit(solution)/shard_map/update/pallas_call | solution.py:505
  186.4 0.0 copy-done
  186.4 0.7 copy.6
Async XLA Ops:
  176.8 9.6 %copy-start = (f32[64,576]{1,0:T(8,128)S(1)}, f32[64,576]{1,0:T(8,128)}, u32[]{:S(2)}) copy-start(f32[64,576]{1,0:T(8,128)} %get-tuple-element.11) | copy-start | bytes 442372

commit v4 on v3

--- a/solution.py
+++ b/solution.py
@@ -96,7 +96,7 @@
             copy.wait_send()
 
 
-NSEM = 160
+NSEM = 200
 
 
 class PlaneGather:
@@ -162,9 +162,17 @@
         other = self.buf.at[(me.row + 4) % 8]
         self.near2 = [self.links.push(other, other, me.xd(d)) for d in (1, 2, 3)]
 
+    def finish_near(self):
+        for copy in self.near:
+            copy.wait_recv()
+
+    def finish_far(self):
+        for copy in self.near2:
+            copy.wait_recv()
+
     def finish(self):
-        for copy in self.near + self.near2:
-            copy.wait_recv()
+        self.finish_near()
+        self.finish_far()
 
 
 def barrier(me):
@@ -268,64 +276,104 @@
     xg.step()
     gg.start()
     lane = lax.broadcasted_iota(jnp.int32, (288, 128), 1)
-    xg.finish()
+
+    def assemble(h):
+        group = zh if h == 0 else 1 - zh
+        for m in range(2):
+            b0, b1 = xbuf[4 * group + 2 * m], xbuf[4 * group + 2 * m + 1]
+            cols = pl.ds(128 * m, 128)
+            xc_hi[h, 0:288, cols], xc_lo[h, 0:288, cols] = split(jnp.where(lane < 64, b0, pltpu.roll(b1, 64, 1)))
+            xc_hi[h, 288:576, cols], xc_lo[h, 288:576, cols] = split(jnp.where(lane < 64, pltpu.roll(b0, 64, 1), b1))
+
+    y1, y2, y3 = (y + 1) % 4, (y + 2) % 4, (y + 3) % 4
+
+    class Half:
+        def __init__(self, h):
+            self.h = h
+
+        def multiply(self, ay):
+            h = self.h
+
+            @pl.loop(0, 2)
+            def _(z):
+                rows = pl.ds(pl.multiple_of(ay * 576 + z * 288, 288), 288)
+                product = dot3(p_hi[rows], p_lo[rows], xc_hi[h], xc_lo[h])
+                part[h, ay, pl.ds(z * 2, 2)] = product.reshape(2, 2, 72, 256)
+
+            return links.push(part.at[h, ay, :, 1 - k], d2d.at[h, ay], me.sib())
+
+        def add_pair(self, ay, copy):
+            h = self.h
+            copy.wait_recv()
+
+            @pl.loop(0, 4)
+            def _(z):
+                csum[h, ay, z] = part[h, ay, z, k] + d2d[h, ay, z]
+
+        def first(self):
+            h = self.h
+            c2 = self.multiply(y2)
+            c1 = self.multiply(y1)
+            self.add_pair(y2, c2)
+            self.up = links.push(csum.at[h, y2, pl.ds(0, 2)], r1.at[h, 0], me.yd(1))
+            self.down = links.push(csum.at[h, y2, pl.ds(2, 2)], r1.at[h, 1], me.yd(3))
+            c3 = self.multiply(y3)
+            self.add_pair(y1, c1)
+            self.c0 = self.multiply(y)
+            self.add_pair(y3, c3)
+
+        def second(self):
+            h = self.h
+            self.up.wait_recv()
+            for z in range(2):
+                csum[h, y1, z] += r1[h, 0, z]
+            self.up2 = links.push(csum.at[h, y1], r2.at[h, 0], me.yd(1))
+            self.down.wait_recv()
+            for z in range(2):
+                csum[h, y3, z + 2] += r1[h, 1, z]
+            self.down2 = links.push(csum.at[h, y3], r2.at[h, 1], me.yd(3))
+            self.add_pair(y, self.c0)
+
+        def third(self):
+            h = self.h
+            self.up2.wait_recv()
+            self.down2.wait_recv()
+
+            @pl.loop(0, 4)
+            def _(z):
+                csum[h, y, z] = csum[h, y, z] + (r2[h, 0, z] + r2[h, 1, z])
+
+            self.zc = [links.push(csum.at[h, y, (zl + d) % 4], rz.at[h, d - 1], me.zd(d)) for d in (1, 2, 3)]
+
+        def last(self):
+            h = self.h
+            for copy in self.zc:
+                copy.wait_recv()
+            group = zh if h == 0 else 1 - zh
+            cols = pl.ds(pl.multiple_of(group * 256, 256), 256)
+            ybuf[y, zl, k, :, cols] = csum[h, y, zl] + rz[h, 0] + (rz[h, 1] + rz[h, 2])
+
+    near, far = Half(0), Half(1)
+    xg.finish_near()
+    assemble(0)
+    near.first()
+    xg.finish_far()
     base_s, base_r = links.slot(8), links.slot(8)
     for q in range(8):
         LooseCopy(links, xp_ref.at[pl.ds(72 * (q % 4), 72)], xs.at[row], me.strip(q), base_s + q, base_r + row)
-    for m in range(4):
-        b0, b1 = xbuf[2 * m], xbuf[2 * m + 1]
-        cols = pl.ds(128 * m, 128)
-        xc_hi[0:288, cols], xc_lo[0:288, cols] = split(jnp.where(lane < 64, b0, pltpu.roll(b1, 64, 1)))
-        xc_hi[288:576, cols], xc_lo[288:576, cols] = split(jnp.where(lane < 64, pltpu.roll(b0, 64, 1), b1))
-
-    def multiply(ay):
-        @pl.loop(0, 2)
-        def _(z):
-            rows = pl.ds(pl.multiple_of(ay * 576 + z * 288, 288), 288)
-            part[ay, pl.ds(z * 2, 2)] = dot3(p_hi[rows], p_lo[rows], xc_hi[...], xc_lo[...]).reshape(2, 2, 72, 512)
-
-        return links.push(part.at[ay, :, 1 - k], d2d.at[ay], me.sib())
-
-    def add_pair(ay, copy):
-        copy.wait_recv()
-
-        @pl.loop(0, 4)
-        def _(z):
-            csum[ay, z] = part[ay, z, k] + d2d[ay, z]
-
-    y1, y2, y3 = (y + 1) % 4, (y + 2) % 4, (y + 3) % 4
-    c2 = multiply(y2)
-    c1 = multiply(y1)
-    add_pair(y2, c2)
-    up = links.push(csum.at[y2, pl.ds(0, 2)], r1.at[0], me.yd(1))
-    down = links.push(csum.at[y2, pl.ds(2, 2)], r1.at[1], me.yd(3))
-    c3 = multiply(y3)
-    add_pair(y1, c1)
-    c0 = multiply(y)
-    add_pair(y3, c3)
-    up.wait_recv()
-    for z in range(2):
-        csum[y1, z] += r1[0, z]
-    up2 = links.push(csum.at[y1], r2.at[0], me.yd(1))
-    down.wait_recv()
-    for z in range(2):
-        csum[y3, z + 2] += r1[1, z]
-    down2 = links.push(csum.at[y3], r2.at[1], me.yd(3))
-    add_pair(y, c0)
+    near.second()
+    assemble(1)
+    far.first()
+    near.third()
+    far.second()
+    near.last()
 
     def gp_multiply(ay, copy):
         copy.wait_recv()
         g_hi, g_lo = split(gbuf[ay].reshape(128, 2304))
         gpp[pl.ds(2 * (ay % 2), 2), ay // 2] = dot3(g_hi, g_lo, p_hi[...], p_lo[...]).reshape(2, 64, 576)
 
-    up2.wait_recv()
-    down2.wait_recv()
-
-    @pl.loop(0, 4)
-    def _(z):
-        csum[y, z] = csum[y, z] + (r2[0, z] + r2[1, z])
-
-    zc = [links.push(csum.at[y, (zl + d) % 4], rz.at[d - 1], me.zd(d)) for d in (1, 2, 3)]
+    far.third()
     gg.step1()
 
     for r in range(8):
@@ -338,9 +386,7 @@
         second = jnp.where(lane72 < 64, pltpu.roll(b0, 64, 1), b1)
         x72[:, 128 * m:128 * m + 128] = jnp.where(flip, second, first)
     gp_multiply(y, gg.own)
-    for copy in zc:
-        copy.wait_recv()
-    ybuf[y, zl, k] = csum[y, zl] + rz[0] + (rz[1] + rz[2])
+    far.last()
 
     yv = ybuf[y, zl, k]
     for i, (top, left) in enumerate(((0, 0), (128, 0), (128, 256), (0, 128))):
@@ -420,7 +466,9 @@
     gcopy.wait_recv()
     gp64[...] = gps[zh] + gpa[...]
     gp_hi, gp_lo = split(gp64[...])
-    gyp[...] = dot3(gp_hi, gp_lo, xc_hi[...], xc_lo[...]).reshape(2, 4, 8, 512)
+    for h in range(2):
+        cols = pl.ds(pl.multiple_of((zh if h == 0 else 1 - zh) * 256, 256), 256)
+        gyp[:, :, :, cols] = dot3(gp_hi, gp_lo, xc_hi[h], xc_lo[h]).reshape(2, 4, 8, 256)
     copy = links.push(gyp.at[1 - k], gyd, me.sib())
     copy.wait_recv()
     gya[...] = gyp[k] + gyd[...]
@@ -461,9 +509,9 @@
     vm = lambda *shape, dtype=F32: pltpu.VMEM(shape, dtype)
     scratch = [
         vm(576, 2304), vm(2304, 576, dtype=BF16), vm(2304, 576, dtype=BF16),
-        vm(8, 288, 128), vm(8, 72, 128), vm(576, 512, dtype=BF16), vm(576, 512, dtype=BF16),
-        vm(4, 4, 2, 16, 2304), vm(4, 4, 2, 72, 512), vm(4, 4, 72, 512), vm(4, 4, 72, 512),
-        vm(2, 2, 72, 512), vm(2, 4, 72, 512), vm(3, 72, 512),
+        vm(8, 288, 128), vm(8, 72, 128), vm(2, 576, 256, dtype=BF16), vm(2, 576, 256, dtype=BF16),
+        vm(4, 4, 2, 16, 2304), vm(2, 4, 4, 2, 72, 256), vm(2, 4, 4, 72, 256), vm(2, 4, 4, 72, 256),
+        vm(2, 2, 2, 72, 256), vm(2, 2, 4, 72, 256), vm(2, 3, 72, 256),
         vm(4, 4, 2, 72, 512), vm(8, 72, 512), vm(72, 512),
         vm(2, 4, 4, 8, 640), vm(4, 4, 8, 640), vm(4, 4, 8, 640), vm(3, 4, 8, 640),
         vm(4, 8, 640), vm(3, 8, 640), vm(2, 8, 640), vm(4, 8, 640), vm(2, 4, 4, 8, 640), vm(512, 512),

time: 187 us -> 178 us (0.952)
  Pallas kernels: 186 us -> 176 us
    pallas_call x1, Pallas kernels: 176 us -> 167 us  [mega_call(): pl.pallas_call(mega, out_shape=[jax.ShapeDtypeStruct((4, 4, 2, 72, 512),...]
where the time goes in v4:
time: 178 us
  Pallas kernels  176 us (99%)
    pallas_call x1, Pallas kernels, mega_call(): pl.pallas_call(mega, out_shape=[jax.ShapeDtypeStruct((4, 4, 2, 72, 512),...  167 us
    pallas_call x1, Pallas kernels, update_call(): pl.pallas_call(update_kernel, grid=(2304 // block,), out_shape=jax.ShapeD...  9.57 us

profile of v4, /device:TPU:1, one launch (start us, length us, event | category | flops | bytes accessed | tf_op | source)
XLA Modules:
  0.0 177.7 jit_solution(14821031538885760327)
XLA Ops:
  0.6 166.8 %solve.1 = (f32[4,4,2,72,512]{4,3,2,1,0:T(8,128)}, f32[576,512]{1,0:T(8,128)}, f32[64,576]{1,0:T(8,128)}) custom-call(f32[576,2304]{1,0:T(8,128)} %bitcast.4, f32[64,576]{1,0:T(8,128)} %bitcast.8, f32[16,2304]{1,0:T(8,128)} %g_ref.1), custom_call_target="tpu_custom_call" | custom-call | tf_op jit(solution)/shard_map/solve/pallas_call | solution.py:524
  167.5 0.0 copy-start
  167.5 9.6 %update.1 = f32[576,2304]{1,0:T(8,128)} custom-call(f32[576,2304]{1,0:T(8,128)} %bitcast.5, f32[2304,512]{1,0:T(8,128)} %bitcast.7, f32[576,512]{1,0:T(8,128)} %get-tuple-element.6.wt_ref), custom_call_target="tpu_custom_call" | custom-call | tf_op jit(solution)/shard_map/update/pallas_call | solution.py:553
  177.1 0.0 copy-done
  177.1 0.7 copy.6
Async XLA Ops:
  167.5 9.6 %copy-start = (f32[64,576]{1,0:T(8,128)S(1)}, f32[64,576]{1,0:T(8,128)}, u32[]{:S(2)}) copy-start(f32[64,576]{1,0:T(8,128)} %get-tuple-element.11) | copy-start | bytes 442372

commit v5 on v4

--- a/solution.py
+++ b/solution.py
@@ -387,6 +387,7 @@
         x72[:, 128 * m:128 * m + 128] = jnp.where(flip, second, first)
     gp_multiply(y, gg.own)
     far.last()
+    yc = LooseCopy(links, ybuf.at[y, zl, k], ycb.at[col % 8], me.strip_source(col % 8), links.slot(), links.slot())
 
     yv = ybuf[y, zl, k]
     for i, (top, left) in enumerate(((0, 0), (128, 0), (128, 256), (0, 128))):
@@ -425,8 +426,10 @@
     for copy in cs:
         copy.wait_recv()
     copy = links.push(gout.at[k], gout.at[k], me.sib())
-    yc = LooseCopy(links, ybuf.at[y, zl, k], ycb.at[col % 8], me.strip_source(col % 8), links.slot(), links.slot())
     gpc = [links.push(gpp.at[(x + d) % 4], gpx.at[d - 1], me.xd(d)) for d in (1, 2, 3)]
+    yc.remote.wait_recv()
+    ycg = RowGather(links, ycb)
+    ycg.start()
     yg.step1()
     copy.wait_recv()
 
@@ -452,17 +455,15 @@
         amat[at, at] = inv
 
     pl.loop(0, 1)(eliminate)
-    yc.remote.wait_recv()
-    ycg = RowGather(links, ycb)
-    ycg.start()
     yg.step2()
+    ycg.step()
+    pl.loop(1, 2)(eliminate)
+    yg.step3()
     for copy in gpc:
         copy.wait_recv()
     gps[...] = gpp[x] + gpx[0] + (gpx[1] + gpx[2])
     gcopy = links.push(gps.at[1 - zh], gpa, me.anti())
-    pl.loop(1, 2)(eliminate)
-    ycg.step()
-    yg.step3()
+    pl.loop(2, 3)(eliminate)
     gcopy.wait_recv()
     gp64[...] = gps[zh] + gpa[...]
     gp_hi, gp_lo = split(gp64[...])
@@ -473,23 +474,19 @@
     copy.wait_recv()
     gya[...] = gyp[k] + gyd[...]
     cs = [links.push(gya.at[(y + d) % 4], gyy.at[d - 1], me.yd(d)) for d in (1, 2, 3)]
-    pl.loop(2, 3)(eliminate)
-    for copy in cs:
-        copy.wait_recv()
-    gyb[...] = gya[y] + gyy[0] + (gyy[1] + gyy[2])
-    cs = [links.push(gyb, gyz.at[d - 1], me.zd(d)) for d in (1, 2, 3)]
     yg.finish()
     out = pltpu.make_async_copy(ybuf, yr_hbm, lsem.at[1])
     out.start()
+    pl.loop(3, 4)(eliminate)
+    for copy in cs:
+        copy.wait_recv()
+    gyb[...] = gya[y] + gyy[0] + (gyy[1] + gyy[2])
+    cs = [links.push(gyb, gyz.at[d - 1], me.zd(d)) for d in (1, 2, 3)]
+    ycg.finish()
     for copy in cs:
         copy.wait_recv()
     gyo[k, y] = gyb[...] + gyz[0] + (gyz[1] + gyz[2])
     cs = [links.push(gyo.at[k, y], gyo.at[k, y], me.yd(d)) for d in (1, 2, 3)]
-    pl.loop(3, 4)(eliminate)
-    for copy in cs:
-        copy.wait_recv()
-    ycopy = links.push(gyo.at[k], gyo.at[k], me.sib())
-    ycg.finish()
     s_hi, s_lo = split(amat[...])
 
     @pl.loop(0, 2)
@@ -497,6 +494,9 @@
         b_hi, b_lo = split(ycb[pl.ds(i * 4, 4)].reshape(288, 512))
         wt_ref[pl.ds(pl.multiple_of(i * 288, 288), 288), :] = dot3(b_hi, b_lo, s_hi, s_lo)
 
+    for copy in cs:
+        copy.wait_recv()
+    ycopy = links.push(gyo.at[k], gyo.at[k], me.sib())
     ycopy.wait_recv()
     gy_hi, gy_lo = split(gyo[...].reshape(64, 512))
     w_hi, w_lo = split(wt_ref[...])

time: 178 us -> 181 us (1.017)
  Pallas kernels: 176 us -> 179 us
    pallas_call x1, Pallas kernels: 167 us -> 170 us  [mega_call(): pl.pallas_call(mega, out_shape=[jax.ShapeDtypeStruct((4, 4, 2, 72, 512),...]
where the time goes in v5:
time: 181 us
  Pallas kernels  179 us (99%)
    pallas_call x1, Pallas kernels, mega_call(): pl.pallas_call(mega, out_shape=[jax.ShapeDtypeStruct((4, 4, 2, 72, 512),...  170 us
    pallas_call x1, Pallas kernels, update_call(): pl.pallas_call(update_kernel, grid=(2304 // block,), out_shape=jax.ShapeD...  9.57 us

profile of v5, /device:TPU:1, one launch (start us, length us, event | category | flops | bytes accessed | tf_op | source)
XLA Modules:
  0.0 180.5 jit_solution(694051302436285986)
XLA Ops:
  0.6 169.6 %solve.1 = (f32[4,4,2,72,512]{4,3,2,1,0:T(8,128)}, f32[576,512]{1,0:T(8,128)}, f32[64,576]{1,0:T(8,128)}) custom-call(f32[576,2304]{1,0:T(8,128)} %bitcast.4, f32[64,576]{1,0:T(8,128)} %bitcast.8, f32[16,2304]{1,0:T(8,128)} %g_ref.1), custom_call_target="tpu_custom_call" | custom-call | tf_op jit(solution)/shard_map/solve/pallas_call | solution.py:524
  170.3 0.0 copy-start
  170.3 9.6 %update.1 = f32[576,2304]{1,0:T(8,128)} custom-call(f32[576,2304]{1,0:T(8,128)} %bitcast.5, f32[2304,512]{1,0:T(8,128)} %bitcast.7, f32[576,512]{1,0:T(8,128)} %get-tuple-element.6.wt_ref), custom_call_target="tpu_custom_call" | custom-call | tf_op jit(solution)/shard_map/update/pallas_call | solution.py:553
  179.9 0.0 copy-done
  179.9 0.7 copy.6
Async XLA Ops:
  170.3 9.6 %copy-start = (f32[64,576]{1,0:T(8,128)S(1)}, f32[64,576]{1,0:T(8,128)}, u32[]{:S(2)}) copy-start(f32[64,576]{1,0:T(8,128)} %get-tuple-element.11) | copy-start | bytes 442372
